TPU v7x, 256 devices: a whole 4x4x8 slice. The times are simulated.
256 devices in a mesh: lon: 32 (over z, y_hi, core), lat: 8 (over y_lo, x).
Axes of the slice: x: 4, y: 4 (y_hi: 2, y_lo: 2; y = y_hi * 2 + y_lo), z: 8, core: 2. Of those that a mesh axis runs over, the one named last changes fastest.
Arguments:
- zonal_current: float32 [48, 512, 4096], P(None, 'lat', 'lon'), may hold values from -6 to 6
- meridional_current: float32 [48, 512, 4096], P(None, 'lat', 'lon'), may hold values from -6 to 6
- heat_anomaly: float32 [48, 512, 4096], P(None, 'lat', 'lon'), may hold values from -6 to 6
- saltiness_anomaly: float32 [48, 512, 4096], P(None, 'lat', 'lon'), may hold values from -6 to 6
- submerged_strata_number: int32 [512, 4096], P('lat', 'lon'), may hold values from 0 to 48
Outputs:
- next_zonal_current: float32 [48, 512, 4096], P(None, 'lat', 'lon')
- next_meridional_current: float32 [48, 512, 4096], P(None, 'lat', 'lon')
- next_heat_anomaly: float32 [48, 512, 4096], P(None, 'lat', 'lon')
- next_saltiness: float32 [48, 512, 4096], P(None, 'lat', 'lon')
All inputs are finite; a program needn't handle non-finite values.
Results may differ from a plain program's by a relative error of at most 0.0003.
Values sent between devices are 32-bit elements; how exact they have to be, the bound alone decides.
No kernel may reach another device: no remote copies, remote signals or barrier semaphores. Data moves between devices by JAX's collectives and lax.ppermute only.
A program may use at most 128 MiB of HBM per device.

v0:
```python
import math

import jax
import jax.numpy as jnp
from jax import lax
from jax.sharding import PartitionSpec as P

time_step = 0.1


def from_partner(block, axis, stride):
    count = lax.axis_size(axis)
    route = []
    for low in range(count):
        high = low | 1 << stride
        if high != low and high < count:
            route += [(low, high), (high, low)]
    return lax.ppermute(block, axis, route)


def padded_2(cells, sides, width, closed):
    for axis, dim in sides:
        count = lax.axis_size(axis)
        ends = count if closed else count - 1
        head = lax.slice_in_dim(cells, 0, width, axis=dim)
        tail = lax.slice_in_dim(cells, cells.shape[dim] - width, cells.shape[dim], axis=dim)
        cells = jnp.concatenate(
            [
                lax.ppermute(tail, axis, [(i, (i + 1) % count) for i in range(ends)]),
                cells,
                lax.ppermute(head, axis, [((i + 1) % count, i) for i in range(ends)]),
            ],
            axis=dim,
        )
    return cells


def centre(values):
    return values[..., 1:-1, 1:-1]


def to_east(values):
    return values[..., 1:-1, 2:]


def to_west(values):
    return values[..., 1:-1, :-2]


def to_north(values):
    return values[..., 2:, 1:-1]


def to_south(values):
    return values[..., :-2, 1:-1]


def column_geometry(stratum_positions):
    layer_number = jnp.arange(stratum_positions).astype(jnp.float32)
    stratum_span = 1.0 + layer_number / stratum_positions
    stratum_centre_height = jnp.cumsum(stratum_span) - 0.5 * stratum_span
    return (stratum_span[:, None, None], stratum_centre_height[:, None, None])


def weight_of_water_above(
    temp_vals, salt_vals, seawater_indicator, stratum_span, stratum_centre_height
):
    density = seawater_indicator * (
        -0.6 * temp_vals
        - 0.1 * temp_vals * temp_vals
        + 0.8 * salt_vals
        + 0.03 * stratum_centre_height * temp_vals
    )
    weight = density * stratum_span
    return jnp.cumsum(weight, axis=0) - 0.5 * weight


def latitude_terms(first_row, parallels_in_block, total_rows):
    row_index = (first_row + jnp.arange(parallels_in_block)).astype(jnp.float32)
    latitude = (-75.0 + 150.0 * (row_index + 0.5) / total_rows) * (math.pi / 180.0)
    return ((1.0 / jnp.cos(latitude))[:, None], (1.5 * jnp.sin(latitude))[:, None])


def advance(zonal_ext, merid_ext, temp_ext, salt_ext, press_ext, wet_ext, inv_dx, coriolis):
    seawater_indicator = centre(wet_ext)
    wet_east = seawater_indicator * to_east(wet_ext)
    wet_west = seawater_indicator * to_west(wet_ext)
    wet_north = seawater_indicator * to_north(wet_ext)
    wet_south = seawater_indicator * to_south(wet_ext)
    zonal_mid = centre(zonal_ext)
    merid_mid = centre(merid_ext)
    flow_east = wet_east * 0.5 * (zonal_mid + to_east(zonal_ext))
    flow_west = wet_west * 0.5 * (zonal_mid + to_west(zonal_ext))
    flow_north = wet_north * 0.5 * (merid_mid + to_north(merid_ext))
    flow_south = wet_south * 0.5 * (merid_mid + to_south(merid_ext))

    def divergence(values):
        middle = centre(values)
        zonal_flux = flow_east * 0.5 * (middle + to_east(values)) - flow_west * 0.5 * (
            middle + to_west(values)
        )
        merid_flux = flow_north * 0.5 * (middle + to_north(values)) - flow_south * 0.5 * (
            middle + to_south(values)
        )
        return zonal_flux * inv_dx + merid_flux

    slope_x = wet_east * wet_west * (to_east(press_ext) - to_west(press_ext)) * 0.5 * inv_dx
    slope_y = wet_north * wet_south * (to_north(press_ext) - to_south(press_ext)) * 0.5
    zonal_new = seawater_indicator * (
        zonal_mid + time_step * (coriolis * merid_mid - slope_x - divergence(zonal_ext))
    )
    merid_new = seawater_indicator * (
        merid_mid + time_step * (-coriolis * zonal_mid - slope_y - divergence(merid_ext))
    )
    temp_new = seawater_indicator * (centre(temp_ext) - time_step * divergence(temp_ext))
    salt_new = seawater_indicator * (centre(salt_ext) - time_step * divergence(salt_ext))
    return (zonal_new, merid_new, temp_new, salt_new)


def mirror_row(top_row):
    mirror_piece = top_row
    for bit_place in range(lax.axis_size("lon").bit_length() - 1):
        mirror_piece = from_partner(mirror_piece, "lon", bit_place)
    return jnp.flip(mirror_piece, axis=1)


def extend_tile(stacked, fold_signs):
    widened = padded_2(stacked, (("lon", 2),), 1, True)
    mirrored = mirror_row(widened[:, -1, :]) * fold_signs[:, None]
    padded = padded_2(widened, (("lat", 1),), 1, False)
    is_top = lax.axis_index("lat") == lax.axis_size("lat") - 1
    new_row = jnp.where(is_top, mirrored, padded[:, -1, :])
    return padded.at[:, -1, :].set(new_row)


def shards(
    zonal_current, meridional_current, heat_anomaly, saltiness_anomaly, submerged_strata_number
):
    stratum_positions, parallels_in_block, zonal_positions = heat_anomaly.shape
    stratum_span, stratum_centre_height = column_geometry(stratum_positions)
    layer_index = jnp.arange(stratum_positions).astype(jnp.float32)[:, None, None]
    kmt_float = submerged_strata_number.astype(jnp.float32)
    seawater_indicator = (layer_index < kmt_float[None]).astype(jnp.float32)
    owned_parallels = [zonal_current, meridional_current, heat_anomaly, saltiness_anomaly]
    owned_parallels.append(
        weight_of_water_above(
            heat_anomaly, saltiness_anomaly, seawater_indicator, stratum_span, stratum_centre_height
        )
    )
    owned_parallels.append(kmt_float[None])
    stacked = jnp.concatenate(owned_parallels, axis=0)
    fold_signs = jnp.concatenate(
        [
            -jnp.ones((2 * stratum_positions,), jnp.float32),
            jnp.ones((stacked.shape[0] - 2 * stratum_positions,), jnp.float32),
        ]
    )
    extended = extend_tile(stacked, fold_signs)
    zonal_ext = extended[:stratum_positions]
    merid_ext = extended[stratum_positions : 2 * stratum_positions]
    temp_ext = extended[2 * stratum_positions : 3 * stratum_positions]
    salt_ext = extended[3 * stratum_positions : 4 * stratum_positions]
    kmt_ext = extended[-1]
    wet_ext = (layer_index < kmt_ext[None]).astype(jnp.float32)
    press_ext = extended[4 * stratum_positions : 5 * stratum_positions]
    inv_dx, coriolis = latitude_terms(
        lax.axis_index("lat") * parallels_in_block,
        parallels_in_block,
        parallels_in_block * lax.axis_size("lat"),
    )
    return advance(zonal_ext, merid_ext, temp_ext, salt_ext, press_ext, wet_ext, inv_dx, coriolis)


def solution(mesh):
    return jax.shard_map(
        shards,
        mesh=mesh,
        in_specs=(
            P(None, "lat", "lon"),
            P(None, "lat", "lon"),
            P(None, "lat", "lon"),
            P(None, "lat", "lon"),
            P("lat", "lon"),
        ),
        out_specs=(
            P(None, "lat", "lon"),
            P(None, "lat", "lon"),
            P(None, "lat", "lon"),
            P(None, "lat", "lon"),
        ),
        check_vma=False,
    )
```

profile of v0, /device:TPU:8, one launch (start us, length us, event | category | flops | bytes accessed | tf_op | source)
XLA Modules:
  0.0 156.7 jit_solution(8544845660575988014)
XLA Ops:
  0.7 0.1 reduce-window.8
  0.7 0.1 reduce.2
  0.9 0.0 copy-start.8
  0.9 0.0 copy-start.7
  0.9 1.6 %constant_dynamic-update-slice_fusion.3 = f32[241,64,128]{2,1,0:T(8,128)S(1)} fusion(f32[48,64,128]{2,1,0:T(8,128)} %param.7), kind=kLoop, calls=%fused_computation.91 | loop fusion | bytes 3145728
  2.5 0.2 copy-done.7
  2.8 0.1 constant_dynamic-update-slice_fusion.2
  2.9 1.3 copy-done.5
  4.2 0.1 constant_dynamic-update-slice_fusion.1
  4.3 1.3 copy-done.6
  5.6 0.1 constant_dynamic-update-slice_fusion
  5.7 1.1 subtract_dynamic-update-slice_fusion
  6.8 7.5 %fusion.54 = (f32[241,64,1]{2,1,0:T(8,128)}, f32[241,64,1]{2,1,0:T(8,128)}) fusion(f32[241,64,128]{2,1,0:T(8,128)S(1)} %bitcast_dynamic-update-slice_fusion), kind=kLoop, calls=%fused_computation.101 | loop fusion | bytes 246784 | tf_op jit(solution)/shard_map/slice | solution.py:26
  14.2 0.4 copy-done
  14.7 5.3 %copy.24 = f32[241,64,1]{0,1,2:T(8,128)S(1)} copy(f32[241,64,1]{2,1,0:T(8,128)} %get-tuple-element.23) | data formatting | bytes 123392 | tf_op jit(solution)/shard_map/slice | solution.py:26
  20.0 0.1 collective-permute-start
  20.1 5.3 %copy.25 = f32[241,64,1]{0,1,2:T(8,128)S(1)} copy(f32[241,64,1]{2,1,0:T(8,128)} %get-tuple-element.24) | data formatting | bytes 123392 | tf_op jit(solution)/shard_map/slice | solution.py:25
  25.4 7.1 %collective-permute-start.1 = (f32[241,64,1]{0,1,2:T(8,128)S(1)}, f32[241,64,1]{0,1,2:T(8,128)S(1)}, u32[]{:S(2)}, u32[]{:S(2)}) collective-permute-start(f32[241,64,1]{0,1,2:T(8,128)S(1)} %copy.25), channel_id=1, source_target_pairs={{8,0},{16,8},{24,16},{32,24},{40,32},{48,40},{56,48},{64,56},{72,6... | collective-permute-start | bytes 185096 | tf_op jit(solution)/shard_map/ppermute | solution.py:31
  32.5 5.0 %copy.26 = f32[241,64,1]{2,1,0:T(8,128)} copy(f32[241,64,1]{0,1,2:T(8,128)S(1)} %collective-permute-done) | data formatting | bytes 123392 | tf_op jit(solution)/shard_map/ppermute | solution.py:29
  37.5 0.0 collective-permute-done.1
  37.5 4.9 %copy.27 = f32[241,64,1]{2,1,0:T(8,128)} copy(f32[241,64,1]{0,1,2:T(8,128)S(1)} %collective-permute-done.1) | data formatting | bytes 123392 | tf_op jit(solution)/shard_map/ppermute | solution.py:31
  42.4 4.4 %pad_maximum_fusion.3 = (f32[241,1,130]{2,1,0:T(1,128)S(1)}, f32[241,1,130]{2,1,0:T(1,128)S(1)}) fusion(f32[241,64,1]{2,1,0:T(8,128)} %copy.27, f32[241,64,128]{2,1,0:T(8,128)} %copy-done, f32[241,64,1]{2,1,0:T(8,128)} %copy.26), kind=kLoop, calls=%fused_computation.82 | loop fusion | flops 125320 | bytes 8271120 | tf_op jit(solution)/shard_map/slice | solution.py:26
  46.8 0.1 copy.28
  46.9 0.1 collective-permute-start.4
  47.0 1.3 collective-permute-done.4
  48.3 0.0 collective-permute-start.5
  48.4 7.2 %collective-permute-done.5 = f32[241,130]{0,1:T(8,128)S(1)} collective-permute-done((f32[241,130]{0,1:T(8,128)S(1)}, f32[241,130]{0,1:T(8,128)S(1)}, u32[]{:S(2)}, u32[]{:S(2)}) %collective-permute-start.5) | collective-permute-done | bytes 125352 | tf_op jit(solution)/shard_map/ppermute | solution.py:18
  55.6 0.0 collective-permute-start.6
  55.6 3.4 %collective-permute-start.2 = (f32[241,1,130]{2,1,0:T(1,128)S(1)}, f32[241,1,130]{2,1,0:T(1,128)S(1)}, u32[]{:S(2)}, u32[]{:S(2)}) collective-permute-start(f32[241,1,130]{2,1,0:T(1,128)S(1)} %get-tuple-element.21), channel_id=1, source_target_pairs={{0,1},{1,2},{2,3},{3,4},{4,5},{5,6},{6,7},{8,9},{9,10},{10,11},{11... | collective-permute-start | bytes 375968 | tf_op jit(solution)/shard_map/ppermute | solution.py:29
  59.0 4.6 %collective-permute-start.3 = (f32[241,1,130]{2,1,0:T(1,128)S(1)}, f32[241,1,130]{2,1,0:T(1,128)S(1)}, u32[]{:S(2)}, u32[]{:S(2)}) collective-permute-start(f32[241,1,130]{2,1,0:T(1,128)S(1)} %get-tuple-element.22), channel_id=1, source_target_pairs={{1,0},{2,1},{3,2},{4,3},{5,4},{6,5},{7,6},{9,8},{10,9},{11,10},{12... | collective-permute-start | bytes 375968 | tf_op jit(solution)/shard_map/ppermute | solution.py:31
  63.5 0.0 collective-permute-done.6
  63.5 3.5 %collective-permute-start.7 = (f32[241,130]{0,1:T(8,128)S(1)}, f32[241,130]{0,1:T(8,128)S(1)}, u32[]{:S(2)}, u32[]{:S(2)}) collective-permute-start(f32[241,130]{0,1:T(8,128)S(1)} %collective-permute-done.6), channel_id=1, source_target_pairs={{0,64},{64,0},{8,72},{72,8},{16,80},{80,16},{24,88},{88,24},{32,96... | collective-permute-start | bytes 375968 | tf_op jit(solution)/shard_map/ppermute | solution.py:18
  67.1 0.6 broadcast_multiply_fusion
  67.7 5.1 %collective-permute-done.7 = f32[241,130]{0,1:T(8,128)S(1)} collective-permute-done((f32[241,130]{0,1:T(8,128)S(1)}, f32[241,130]{0,1:T(8,128)S(1)}, u32[]{:S(2)}, u32[]{:S(2)}) %collective-permute-start.7) | collective-permute-done | bytes 125352 | tf_op jit(solution)/shard_map/ppermute | solution.py:18
  72.8 4.8 %collective-permute-start.8 = (f32[241,130]{0,1:T(8,128)S(1)}, f32[241,130]{0,1:T(8,128)S(1)}, u32[]{:S(2)}, u32[]{:S(2)}) collective-permute-start(f32[241,130]{0,1:T(8,128)S(1)} %collective-permute-done.7), channel_id=1, source_target_pairs={{0,128},{128,0},{8,136},{136,8},{16,144},{144,16},{24,152},{152,24... | collective-permute-start | bytes 375968 | tf_op jit(solution)/shard_map/ppermute | solution.py:18
  77.6 19.8 %pad_maximum_fusion = f32[241,66,130]{2,1,0:T(8,128)} fusion(f32[241,1,130]{2,1,0:T(1,128)S(1)} %collective-permute-done.3, f32[241,64,1]{2,1,0:T(8,128)} %copy.27, f32[241,64,128]{2,1,0:T(8,128)} %copy-done, f32[241,64,1]{2,1,0:T(8,128)} %copy.26, f32[241,1,130]{2,1,0:T(1,128)S(1)} %collective-permute-done.2), kind=kLoop, calls=%fused_computation | loop fusion | flops 8271120 | bytes 16542240 | tf_op jit(solution)/shard_map/concatenate | solution.py:27
  97.5 0.1 copy.29
  97.6 0.3 rev.4
  97.9 0.2 copy.30
  98.1 6.8 %scatter.4 = f32[241,66,130]{2,1,0:T(8,128)} dynamic-update-slice(f32[241,66,130]{2,1,0:T(8,128)} %pad_maximum_fusion, f32[241,1,130]{2,1,0:T(1,128)S(1)} %copy.30, s32[]{:T(128)} %constant.72.clone.1, s32[]{:T(128)} %constant.73.clone.1, s32[]{:T(128)} %constant.72.clone.1) | dynamic-update-slice | bytes 250644 | tf_op jit(solution)/shard_map/scatter | solution.py:133
  104.9 0.9 slice_bitcast_fusion
  105.8 0.3 compare_convert_fusion
  106.1 17.2 %fusion.10 = (f32[48,64,128]{2,1,0:T(8,128)}, f32[48,64,128]{2,1,0:T(8,128)}, f32[48,64,128]{2,1,0:T(8,128)}, f32[48,64,128]{2,1,0:T(8,128)}, f32[48,64,128]{2,1,0:T(8,128)}) fusion(f32[241,66,130]{2,1,0:T(8,128)} %scatter.4, f32[48,66,130]{2,1,0:T(8,128)S(1)} %compare_convert_fusion, f32[64]{0:T(128)S(1)} %get-tuple-element.27), kind=kLoop, calls=%fused_computation.14 | loop fusion | flops 13762560 | bytes 33030400 | tf_op jit(solution)/shard_map/mul | solution.py:116
  123.3 0.0 copy-start.1
  123.3 0.0 copy-start.2
  123.3 12.5 %fusion.21 = f32[48,64,128]{2,1,0:T(8,128)} fusion(f32[241,66,130]{2,1,0:T(8,128)} %scatter.4, f32[48,64,128]{2,1,0:T(8,128)} %get-tuple-element.20, f32[48,66,130]{2,1,0:T(8,128)S(1)} %compare_convert_fusion, f32[48,64,128]{2,1,0:T(8,128)} %get-tuple-element.19, f32[48,64,128]{2,1,0:T(8,128)} %get-tuple-element.18, f32[48,64,128]{2,1,0:T(8,128)} %get-tuple-element.17, ...), kind=kLoop, calls=%fused_computation.29 | loop fusion | flops 12189696 | bytes 23593216 | tf_op jit(solution)/shard_map/mul | solution.py:115
  135.9 10.7 %fusion.34 = f32[48,64,128]{2,1,0:T(8,128)} fusion(f32[241,66,130]{2,1,0:T(8,128)} %scatter.4, f32[48,64,128]{2,1,0:T(8,128)S(1)} %copy-done.4, f32[48,64,128]{2,1,0:T(8,128)S(1)} %copy-done.3, f32[48,66,130]{2,1,0:T(8,128)S(1)} %compare_convert_fusion, f32[48,64,128]{2,1,0:T(8,128)S(1)} %copy-done.2, f32[48,64,128]{2,1,0:T(8,128)S(1)} %copy-done.1, ...), kind=kLoop, calls=%fused_computation.46 | loop fusion | flops 14155776 | bytes 25166336 | tf_op jit(solution)/shard_map/mul | solution.py:112
  146.7 10.1 %fusion.45 = f32[48,64,128]{2,1,0:T(8,128)} fusion(f32[241,66,130]{2,1,0:T(8,128)} %scatter.4, f32[48,64,128]{2,1,0:T(8,128)S(1)} %copy-done.4, f32[48,66,130]{2,1,0:T(8,128)S(1)} %compare_convert_fusion, f32[48,64,128]{2,1,0:T(8,128)S(1)} %copy-done.3, f32[48,64,128]{2,1,0:T(8,128)S(1)} %copy-done.2, f32[48,64,128]{2,1,0:T(8,128)S(1)} %copy-done.1, ...), kind=kLoop, calls=%fused_computation.60 | loop fusion | flops 14155776 | bytes 25166592 | tf_op jit(solution)/shard_map/mul | solution.py:109
  (25 shorter events, 0.2 us)
Async XLA Ops:
  0.9 1.7 %copy-start.8 = (s32[64,128]{1,0:T(8,128)S(1)}, s32[64,128]{1,0:T(8,128)}, u32[]{:S(2)}) copy-start(s32[64,128]{1,0:T(8,128)} %param.11) | copy-start | bytes 98308
  0.9 1.9 %copy-start.7 = (f32[48,64,128]{2,1,0:T(8,128)S(1)}, f32[48,64,128]{2,1,0:T(8,128)}, u32[]{:S(2)}) copy-start(f32[48,64,128]{2,1,0:T(8,128)} %param.8) | copy-start | bytes 4718596
  2.8 1.4 copy-start.5
  4.2 1.4 copy-start.6
  6.8 7.9 %copy-start = (f32[241,64,128]{2,1,0:T(8,128)}, f32[241,64,128]{2,1,0:T(8,128)S(1)}, u32[]{:S(2)}) copy-start(f32[241,64,128]{2,1,0:T(8,128)S(1)} %bitcast_dynamic-update-slice_fusion) | copy-start | bytes 23691268
  20.0 12.5 %collective-permute-start = (f32[241,64,1]{0,1,2:T(8,128)S(1)}, f32[241,64,1]{0,1,2:T(8,128)S(1)}, u32[]{:S(2)}, u32[]{:S(2)}) collective-permute-start(f32[241,64,1]{0,1,2:T(8,128)S(1)} %copy.24), channel_id=1, source_target_pairs={{0,8},{8,16},{16,24},{24,32},{32,40},{40,48},{48,56},{56,64},{64,7... | collective-permute-start | bytes 185096 | tf_op jit(solution)/shard_map/ppermute | solution.py:29
  25.4 12.1 %collective-permute-start.1 = (f32[241,64,1]{0,1,2:T(8,128)S(1)}, f32[241,64,1]{0,1,2:T(8,128)S(1)}, u32[]{:S(2)}, u32[]{:S(2)}) collective-permute-start(f32[241,64,1]{0,1,2:T(8,128)S(1)} %copy.25), channel_id=1, source_target_pairs={{8,0},{16,8},{24,16},{32,24},{40,32},{48,40},{56,48},{64,56},{72,6... | collective-permute-start | bytes 185096 | tf_op jit(solution)/shard_map/ppermute | solution.py:31
  46.9 1.4 collective-permute-start.4
  48.3 7.2 %collective-permute-start.5 = (f32[241,130]{0,1:T(8,128)S(1)}, f32[241,130]{0,1:T(8,128)S(1)}, u32[]{:S(2)}, u32[]{:S(2)}) collective-permute-start(f32[241,130]{0,1:T(8,128)S(1)} %collective-permute-done.4), channel_id=1, source_target_pairs={{0,16},{16,0},{8,24},{24,8},{32,48},{48,32},{40,56},{56,40},{64,80... | collective-permute-start | bytes 375968 | tf_op jit(solution)/shard_map/ppermute | solution.py:18
  55.6 8.0 %collective-permute-start.6 = (f32[241,130]{0,1:T(8,128)S(1)}, f32[241,130]{0,1:T(8,128)S(1)}, u32[]{:S(2)}, u32[]{:S(2)}) collective-permute-start(f32[241,130]{0,1:T(8,128)S(1)} %collective-permute-done.5), channel_id=1, source_target_pairs={{0,32},{32,0},{8,40},{40,8},{16,48},{48,16},{24,56},{56,24},{64,96... | collective-permute-start | bytes 375968 | tf_op jit(solution)/shard_map/ppermute | solution.py:18
  55.6 22.1 %collective-permute-start.2 = (f32[241,1,130]{2,1,0:T(1,128)S(1)}, f32[241,1,130]{2,1,0:T(1,128)S(1)}, u32[]{:S(2)}, u32[]{:S(2)}) collective-permute-start(f32[241,1,130]{2,1,0:T(1,128)S(1)} %get-tuple-element.21), channel_id=1, source_target_pairs={{0,1},{1,2},{2,3},{3,4},{4,5},{5,6},{6,7},{8,9},{9,10},{10,11},{11... | collective-permute-start | bytes 375968 | tf_op jit(solution)/shard_map/ppermute | solution.py:29
  59.0 18.7 %collective-permute-start.3 = (f32[241,1,130]{2,1,0:T(1,128)S(1)}, f32[241,1,130]{2,1,0:T(1,128)S(1)}, u32[]{:S(2)}, u32[]{:S(2)}) collective-permute-start(f32[241,1,130]{2,1,0:T(1,128)S(1)} %get-tuple-element.22), channel_id=1, source_target_pairs={{1,0},{2,1},{3,2},{4,3},{5,4},{6,5},{7,6},{9,8},{10,9},{11,10},{12... | collective-permute-start | bytes 375968 | tf_op jit(solution)/shard_map/ppermute | solution.py:31
  63.5 9.3 %collective-permute-start.7 = (f32[241,130]{0,1:T(8,128)S(1)}, f32[241,130]{0,1:T(8,128)S(1)}, u32[]{:S(2)}, u32[]{:S(2)}) collective-permute-start(f32[241,130]{0,1:T(8,128)S(1)} %collective-permute-done.6), channel_id=1, source_target_pairs={{0,64},{64,0},{8,72},{72,8},{16,80},{80,16},{24,88},{88,24},{32,96... | collective-permute-start | bytes 375968 | tf_op jit(solution)/shard_map/ppermute | solution.py:18
  67.7 30.2 %copy-start.9 = (f32[241]{0:T(256)S(1)}, f32[241]{0:T(256)}, u32[]{:S(2)}) copy-start(f32[241]{0:T(256)} %constant.71.clone.1) | copy-start | bytes 2896
  72.8 24.8 %collective-permute-start.8 = (f32[241,130]{0,1:T(8,128)S(1)}, f32[241,130]{0,1:T(8,128)S(1)}, u32[]{:S(2)}, u32[]{:S(2)}) collective-permute-start(f32[241,130]{0,1:T(8,128)S(1)} %collective-permute-done.7), channel_id=1, source_target_pairs={{0,128},{128,0},{8,136},{136,8},{16,144},{144,16},{24,152},{152,24... | collective-permute-start | bytes 375968 | tf_op jit(solution)/shard_map/ppermute | solution.py:18
  123.3 12.6 %copy-start.1 = (f32[48,64,128]{2,1,0:T(8,128)S(1)}, f32[48,64,128]{2,1,0:T(8,128)}, u32[]{:S(2)}) copy-start(f32[48,64,128]{2,1,0:T(8,128)} %get-tuple-element.17) | copy-start | bytes 4718596
  123.3 12.6 %copy-start.2 = (f32[48,64,128]{2,1,0:T(8,128)S(1)}, f32[48,64,128]{2,1,0:T(8,128)}, u32[]{:S(2)}) copy-start(f32[48,64,128]{2,1,0:T(8,128)} %get-tuple-element.18) | copy-start | bytes 4718596
  123.3 12.6 %copy-start.3 = (f32[48,64,128]{2,1,0:T(8,128)S(1)}, f32[48,64,128]{2,1,0:T(8,128)}, u32[]{:S(2)}) copy-start(f32[48,64,128]{2,1,0:T(8,128)} %get-tuple-element.19) | copy-start | bytes 4718596
  123.3 12.6 %copy-start.4 = (f32[48,64,128]{2,1,0:T(8,128)S(1)}, f32[48,64,128]{2,1,0:T(8,128)}, u32[]{:S(2)}) copy-start(f32[48,64,128]{2,1,0:T(8,128)} %get-tuple-element.20) | copy-start | bytes 4718596
  135.9 10.8 %copy-start.10 = (f32[64]{0:T(128)S(1)}, f32[64]{0:T(128)}, u32[]{:S(2)}) copy-start(f32[64]{0:T(128)} %get-tuple-element.29) | copy-start | bytes 772
where the time goes:
time: 157 us
  other arithmetic  76.9 us (49%)
  local copies, waits for them, and re-layouts  41.6 us (26%)
  starting transfers between devices  23.5 us (15%)
  waiting for transfers between devices  13.7 us (9%)
    concatenate x1, other arithmetic, padded_2(): jnp.concatenate([lax.ppermute(tail, axis, [(i, (i + 1) % count) for i in...  19.8 us
    mul x1, other arithmetic, advance(): seawater_indicator * (centre(salt_ext) - time_step * divergence(salt_ext))  17.2 us
    ppermute x5, waiting for transfers between devices, from_partner(): return lax.ppermute(block, axis, route)  13.7 us
    slice x3, local copies, waits for them, and re-layouts, padded_2(): lax.slice_in_dim(cells, cells.shape[dim] - width, cells.shape[dim], axis=...  12.9 us
    mul x1, other arithmetic, advance(): seawater_indicator * (centre(temp_ext) - time_step * divergence(temp_ext))  12.5 us
    ppermute x2, starting transfers between devices, padded_2(): lax.ppermute(head, axis, [((i + 1) % count, i) for i in range(ends)])  11.7 us
    mul x1, other arithmetic, advance(): seawater_indicator * (merid_mid + time_step * (-coriolis * zonal_mid - sl...  10.7 us
    mul x1, other arithmetic, advance(): seawater_indicator * (zonal_mid + time_step * (coriolis * merid_mid - slo...  10.1 us
  transfers between devices with their start and end apart: 9, of which 3 were waited for; matrix products, arithmetic and copies ran while one was open for 20% of the time, Pallas kernels for 0%

commit v1 on v0

v1 whole, which is shorter than its diff:
```python
import math

import jax
import jax.numpy as jnp
from jax import lax
from jax.experimental import pallas as pl
from jax.experimental.pallas import tpu as pltpu
from jax.sharding import PartitionSpec as P

NK, NJ, NI = 48, 64, 128
JT = NJ // 8
NQ = NK // 3
CH = 4
CK = NK // CH
F32 = jnp.float32
VM = pl.BlockSpec(memory_space=pltpu.VMEM)
ANY = pl.BlockSpec(memory_space=pl.ANY)
LIMIT = 48 * 1024 * 1024


def lanes():
    return lax.broadcasted_iota(jnp.int32, (8, NI), 1)


def subs():
    return lax.broadcasted_iota(jnp.int32, (8, NI), 0)


def roll(x, shift, axis):
    return pltpu.roll(x, shift, axis)


def place(k, jt):
    return pl.ds(pl.multiple_of(k * NJ, NJ) + 8 * jt, 8)


def tile(ref, k, jt):
    return ref[place(k, jt), :]


def split_pairs(a, b, even):
    return jnp.where(even, a, roll(b, 1, 1)), jnp.where(even, roll(a, 127, 1), b)


def join_pairs(e, w, even):
    return jnp.where(even, e, roll(w, 1, 1)), jnp.where(even, roll(e, 127, 1), w)


def level_terms(k):
    h = 1.0 + k * (1.0 / NK)
    z = (k + 1.0) + k * (k + 1.0) * (0.5 / NK) - 0.5 * h
    return 0.5 * h * (-0.6 + 0.03 * z), -0.05 * h, 0.4 * h


def packed_latitude():
    row = lax.axis_index("lat") * NJ + (lanes() & 7) * 8 + subs()
    total = NJ * lax.axis_size("lat")
    phi = (-75.0 + 150.0 * (row.astype(F32) + 0.5) / total) * (math.pi / 180.0)
    return 1.0 / jnp.cos(phi), 1.5 * jnp.sin(phi)


def pack_kernel(kmt, u, v, t, s, uo, vo, to, so, near, far, ra, rb, sem):
    copies = [
        [
            pltpu.make_async_copy(
                src.at[pl.ds(c * CK * NJ, CK * NJ)],
                dst.at[pl.ds(c * CK * NJ, CK * NJ)],
                sem.at[c, f],
            )
            for f, (src, dst) in enumerate(((u, uo), (v, vo), (t, to), (s, so)))
        ]
        for c in range(CH)
    ]
    for group in copies:
        for copy in group:
            copy.start()
    lon, lat = lax.axis_index("lon"), lax.axis_index("lat")
    lon_even, lat_even = lon % 2 == 0, lat % 2 == 0
    lane = lanes()
    even = (lane & 1) == 0
    spot = [(lane >> 1) == 60 + jh for jh in range(4)]
    outs = (uo, vo, to, so)

    def put(acc, tiles):
        for jh in range(4):
            acc = jnp.where(spot[jh], roll(tiles[jh], 121 + 2 * jh, 1), acc)
        return acc

    kf = [kmt[8 * jt : 8 * jt + 8, :].astype(F32) for jt in range(JT)]
    inner = [
        jnp.minimum(x, jnp.where(lane == 0, roll(x, 127, 1), roll(x, 1, 1))) for x in kf
    ]
    zero = jnp.zeros((8, NI), F32)
    for at, tiles in ((96, kf), (104, inner)):
        e, w = split_pairs(put(zero, tiles[0::2]), put(zero, tiles[1::2]), even)
        for shift in (8, 16, 32, 64):
            e = e + roll(e, shift, 1)
            w = w + roll(w, shift, 1)
        near[at : at + 8, :] = jnp.where(lon_even, e, w)
        far[at : at + 8, :] = jnp.where(lon_even, w, e)

    def step(q, carry):
        new = []
        for f in range(4):
            for i in range(3):
                k = q * 3 + i
                for half in range(2):
                    acc = roll(carry[f * 6 + i * 2 + half], 120, 1)
                    tiles = [tile(outs[f], k, jt) for jt in range(half, JT, 2)]
                    new.append(put(acc, tiles))
        return tuple(new)

    carry = (zero,) * 24
    for c in range(CH):
        for copy in copies[c]:
            copy.wait()
        carry = lax.fori_loop(c * NQ // CH, (c + 1) * NQ // CH, step, carry)
    for f in range(4):
        for i in range(3):
            e, w = split_pairs(carry[f * 6 + i * 2], carry[f * 6 + i * 2 + 1], even)
            at = (f * 3 + i) * 8
            near[at : at + 8, :] = jnp.where(lon_even, e, w)
            far[at : at + 8, :] = jnp.where(lon_even, w, e)

    fold = lat == lax.axis_size("lat") - 1
    order = jnp.where(fold, 127 - lane, lane)
    tops, bottoms = [], []
    for ref in outs:
        top = ref[pl.ds(NJ - 1, NK, stride=NJ), :]
        bottom = ref[pl.ds(0, NK, stride=NJ), :]
        for b in range(6):
            tops.append(top[8 * b : 8 * b + 8, :])
            bottoms.append(bottom[8 * b : 8 * b + 8, :])
    tops.append(jnp.broadcast_to(kf[JT - 1][7:8, :], (8, NI)))
    bottoms.append(jnp.broadcast_to(kf[0][0:1, :], (8, NI)))
    for n, (top, bottom) in enumerate(zip(tops, bottoms)):
        ra[8 * n : 8 * n + 8, :] = jnp.where(lat_even, top, bottom)
        rb[8 * n : 8 * n + 8, :] = jnp.take_along_axis(
            jnp.where(lat_even, bottom, top), order, axis=1, mode="promise_in_bounds"
        )


def main_kernel(
    kmt, u_ref, v_ref, t_ref, s_ref, ou, ov, ot, os, pin, p62, p1, ks, ke, kn, kew, kns, rs, fs
):
    kf = kmt[...].astype(F32)
    lane64 = lax.broadcasted_iota(jnp.int32, (NJ, NI), 1)
    row64 = lax.broadcasted_iota(jnp.int32, (NJ, NI), 0)
    k_e = jnp.minimum(kf, roll(kf, 127, 1))
    k_w = roll(kf, 1, 1)
    k_n = jnp.minimum(kf, roll(kf, NJ - 1, 0))
    k_s = roll(kf, 1, 0)
    ks[...] = kf
    ke[...] = jnp.where(lane64 == NI - 1, 0.0, k_e)
    kew[...] = jnp.where((lane64 == 0) | (lane64 == NI - 1), 0.0, jnp.minimum(k_e, k_w))
    kn[...] = jnp.where(row64 == NJ - 1, 0.0, k_n)
    kns[...] = jnp.where((row64 == 0) | (row64 == NJ - 1), 0.0, jnp.minimum(k_n, k_s))
    r, f = packed_latitude()
    for jt in range(JT):
        rs[8 * jt : 8 * jt + 8, :] = jnp.broadcast_to(0.025 * r[:, jt : jt + 1], (8, NI))
        fs[8 * jt : 8 * jt + 8, :] = jnp.broadcast_to(0.1 * f[:, jt : jt + 1], (8, NI))

    lane, row = lanes(), subs()
    first, row0, row7 = lane == 0, row == 0, row == 7
    even = (lane & 1) == 0
    spot = [(lane >> 1) == 60 + jh for jh in range(4)]
    zero = jnp.zeros((8, NI), F32)

    def fixed(ref, jt):
        return ref[8 * jt : 8 * jt + 8, :]

    def north(now, after):
        return roll(jnp.where(row0, after, now), 7, 0)

    def south(now, before):
        return roll(jnp.where(row7, before, now), 1, 0)

    def level(k, acc, edge):
        kk = k.astype(F32)
        c1, c2, c3 = level_terms(kk)
        press, acc_new = [], []
        for jt in range(JT):
            t = tile(t_ref, k, jt)
            w = t * (c1 + c2 * t) + c3 * tile(s_ref, k, jt)
            w = jnp.where(fixed(ks, jt) > kk, w, 0.0)
            p = acc[jt] + w
            press.append(p)
            acc_new.append(p + w)
        p62[pl.ds(k, 1), :] = press[JT - 1][6:7, :]
        p1[pl.ds(k, 1), :] = press[0][1:2, :]
        edge = [roll(x, 120, 1) for x in edge]
        before = [zero] * 4
        for jt in range(JT):
            q = [tile(ref, k, jt) for ref in (u_ref, v_ref, t_ref, s_ref)]
            up = min(jt + 1, JT - 1)
            r25, f01 = fixed(rs, jt), fixed(fs, jt)
            qe = [x + roll(x, 127, 1) for x in q]
            flow = jnp.where(fixed(ke, jt) > kk, r25, 0.0) * qe[0]
            fe = [flow * x for x in qe]
            qn = [
                x + north(x, tile(ref, k, up)) for x, ref in zip(q, (u_ref, v_ref, t_ref, s_ref))
            ]
            flow = jnp.where(fixed(kn, jt) > kk, 0.025, 0.0) * qn[1]
            fn = [flow * x for x in qn]
            out = [
                x - (a - roll(a, 1, 1)) - (b - south(b, c))
                for x, a, b, c in zip(q, fe, fn, before)
            ]
            before = fn
            p = press[jt]
            pe, pw = roll(p, 127, 1), roll(p, 1, 1)
            spot_p = roll(jnp.where(first, pe, pw), 121 + 2 * (jt // 2), 1)
            edge[jt % 2] = jnp.where(spot[jt // 2], spot_p, edge[jt % 2])
            slope = jnp.where(fixed(kew, jt) > kk, 2.0 * r25, 0.0) * (pe - pw)
            out[0] = out[0] + (f01 * q[1] - slope)
            pn, ps = north(p, press[up]), south(p, press[max(jt - 1, 0)])
            slope = jnp.where(fixed(kns, jt) > kk, 0.05, 0.0) * (pn - ps)
            out[1] = out[1] - (f01 * q[0] + slope)
            wet = fixed(ks, jt) > kk
            for ref, x in zip((ou, ov, ot, os), out):
                ref[place(k, jt), :] = jnp.where(wet, x, 0.0)
        return acc_new, edge

    def step(q, carry):
        acc = list(carry[:JT])
        edges = list(carry[JT:])
        for i in range(3):
            acc, edges[2 * i : 2 * i + 2] = level(q * 3 + i, acc, edges[2 * i : 2 * i + 2])
        return tuple(acc) + tuple(edges)

    carry = lax.fori_loop(0, NQ, step, (zero,) * (JT + 6))
    for i in range(3):
        e, w = split_pairs(carry[JT + 2 * i], carry[JT + 2 * i + 1], even)
        pin[8 * i : 8 * i + 8, :] = e
        pin[24 + 8 * i : 32 + 8 * i, :] = w


def fix_kernel(
    kmt, u_ref, v_ref, t_ref, s_ref, bu, bv, bt, bs, pin, p62, p1,
    near, far, near_in, far_in, ra_in, rb_in, ou, ov, ot, os, buf, rows, sem,
):
    lon, lat = lax.axis_index("lon"), lax.axis_index("lat")
    lon_even, lat_even = lon % 2 == 0, lat % 2 == 0
    is_top, is_bottom = lat == lax.axis_size("lat") - 1, lat == 0
    lane, row = lanes(), subs()
    even = (lane & 1) == 0
    fields = (u_ref, v_ref, t_ref, s_ref)

    level48 = lax.broadcasted_iota(jnp.int32, (NK, NI), 0).astype(F32)
    row48 = lax.broadcasted_iota(jnp.int32, (NK, NI), 0)
    c1, c2, c3 = level_terms(level48)
    sign = jnp.where(is_top, -1.0, 1.0)
    for side in range(2):
        own_row, next_row = (NJ - 1, NJ - 2) if side == 0 else (0, 1)
        use_a = lat_even if side == 0 else jnp.logical_not(lat_even)
        halo = [
            jnp.where(use_a, ra_in[NK * f : NK * f + NK, :], rb_in[NK * f : NK * f + NK, :])
            for f in range(4)
        ]
        k_halo = jnp.where(use_a, ra_in[4 * NK : 4 * NK + 1, :], rb_in[4 * NK : 4 * NK + 1, :])
        if side == 0:
            halo[0], halo[1] = halo[0] * sign, halo[1] * sign
        else:
            k_halo = jnp.where(is_bottom, 0.0, k_halo)
        own = [
            ref[pl.ds(own_row, NK, stride=NJ), :] for ref in fields
        ]
        k_own = kmt[own_row : own_row + 1, :].astype(F32)
        k_next = kmt[next_row : next_row + 1, :].astype(F32)
        k_face = jnp.minimum(k_own, k_halo)
        w = halo[2] * (c1 + c2 * halo[2]) + c3 * halo[3]
        w = jnp.where(level48 < k_halo, w, 0.0)
        total = w + w
        shift = 1
        while shift < NK:
            total = total + jnp.where(row48 >= shift, roll(total, shift, 0), 0.0)
            shift *= 2
        press = total - w
        flow = jnp.where(level48 < k_face, 0.025, 0.0) * (own[1] + halo[1])
        if side == 0:
            flow = -flow
        slope = press - p62[...] if side == 0 else p1[...] - press
        slope = jnp.where(level48 < jnp.minimum(k_face, k_next), 0.05, 0.0) * slope
        for f in range(4):
            add = flow * (own[f] + halo[f])
            if f == 1:
                add = add - slope
            rows[side, f, :, :] = add

    r, _ = packed_latitude()
    r25 = 0.025 * r
    level_of = [((lane >> 3) * 3 + i).astype(F32) for i in range(3)]
    terms = [level_terms(x) for x in level_of]
    sides = []
    for side in range(2):
        use_near = lon_even if side == 0 else jnp.logical_not(lon_even)

        def block(a, b, at):
            return jnp.where(use_near, a[at : at + 8, :], b[at : at + 8, :])

        k_own, k_in = block(near, far, 96), block(near, far, 104)
        k_halo = block(near_in, far_in, 96)
        k_face = jnp.minimum(k_own, k_halo)
        k_three = jnp.minimum(k_in, k_halo)
        own = [[block(near, far, (f * 3 + i) * 8) for i in range(3)] for f in range(4)]
        halo = [[block(near_in, far_in, (f * 3 + i) * 8) for i in range(3)] for f in range(4)]
        ws = []
        for i in range(3):
            c1, c2, c3 = terms[i]
            w = halo[2][i] * (c1 + c2 * halo[2][i]) + c3 * halo[3][i]
            ws.append(jnp.where(level_of[i] < k_halo, w, 0.0))
        group = 2.0 * (ws[0] + ws[1] + ws[2])
        total = group
        for shift in (8, 16, 32, 64):
            total = total + jnp.where(lane >= shift, roll(total, shift, 1), 0.0)
        above = jnp.where(lane >= 8, roll(total, 8, 1), 0.0)
        corr = [[None] * 3 for _ in range(4)]
        for i in range(3):
            press = above + ws[i]
            above = press + ws[i]
            flow = jnp.where(level_of[i] < k_face, r25, 0.0) * (own[0][i] + halo[0][i])
            inner = pin[24 * side + 8 * i : 24 * side + 8 * i + 8, :]
            slope = press - inner if side == 0 else inner - press
            slope = jnp.where(level_of[i] < k_three, 2.0 * r25, 0.0) * slope
            if side == 0:
                flow = -flow
            for f in range(4):
                corr[f][i] = flow * (own[f][i] + halo[f][i])
            corr[0][i] = corr[0][i] - slope
        sides.append(corr)
    packs = []
    for f in range(4):
        for i in range(3):
            packs += list(join_pairs(sides[0][f][i], sides[1][f][i], even))

    border = (lane == 0) | (lane == NI - 1)
    last_row, first_row = row == 7, row == 0
    bases, outs = (bu, bv, bt, bs), (ou, ov, ot, os)

    def step(q, carry):
        new = []
        for f in range(4):
            for i in range(3):
                k = q * 3 + i
                for half in range(2):
                    pack = carry[f * 6 + i * 2 + half]
                    for jh in range(4):
                        jt = 2 * jh + half
                        x = tile(bases[f], k, jt)
                        x = x + jnp.where(border, roll(pack, 127 - 2 * jh, 1), 0.0)
                        if jt == 0:
                            x = x + jnp.where(first_row, rows[1, f, pl.ds(k, 1), :], 0.0)
                        if jt == JT - 1:
                            x = x + jnp.where(last_row, rows[0, f, pl.ds(k, 1), :], 0.0)
                        buf[f, place(k, jt), :] = x
                    new.append(roll(pack, 120, 1))
        return tuple(new)

    carry = tuple(packs)
    copies = []
    for c in range(CH):
        carry = lax.fori_loop(c * NQ // CH, (c + 1) * NQ // CH, step, carry)
        for f in range(4):
            copy = pltpu.make_async_copy(
                buf.at[f, pl.ds(c * CK * NJ, CK * NJ)],
                outs[f].at[pl.ds(c * CK * NJ, CK * NJ)],
                sem.at[c, f],
            )
            copy.start()
            copies.append(copy)
    for copy in copies:
        copy.wait()


def near_core(x):
    return pltpu.with_memory_space_constraint(x, pltpu.VMEM)


def shards(u, v, t, s, kmt):
    nlon, nlat = lax.axis_size("lon"), lax.axis_size("lat")
    u, v, t, s = (x.reshape(NK * NJ, NI) for x in (u, v, t, s))
    field = jax.ShapeDtypeStruct((NK * NJ, NI), F32)
    params = pltpu.CompilerParams(vmem_limit_bytes=LIMIT)
    vfield = pltpu.VMEM((NK * NJ, NI), F32)
    column = pltpu.VMEM((112, NI), F32)
    strip = pltpu.VMEM((200, NI), F32)
    with jax.named_scope("pack"):
        *held, near, far, ra, rb = pl.pallas_call(
            pack_kernel,
            in_specs=[VM] + [ANY] * 4,
            out_specs=[VM] * 8,
            out_shape=[vfield] * 4 + [column] * 2 + [strip] * 2,
            scratch_shapes=[pltpu.SemaphoreType.DMA((CH, 4))],
            compiler_params=params,
            cost_estimate=pl.CostEstimate(
                flops=4_000_000, bytes_accessed=7_000_000, transcendentals=0
            ),
        )(kmt, u, v, t, s)

    held = [near_core(x) for x in held]

    def device(lon, lat):
        return lon * nlat + lat

    near_route = [(l, l ^ 1) for l in range(nlon)]
    far_route = [(l, (l + (1 if l % 2 else -1)) % nlon) for l in range(nlon)]
    a_route, b_route = [], []
    for l in range(nlon):
        for a in range(nlat):
            a_route.append((device(l, a), device(l, a ^ 1)))
            if a == 0:
                b_route.append((device(l, a), device(l ^ 1, a)))
            elif a == nlat - 1:
                b_route.append((device(l, a), device(nlon - 1 - l, a)))
            else:
                b_route.append((device(l, a), device(l, a + (1 if a % 2 else -1))))
    both = ("lon", "lat")
    with jax.named_scope("halo"):
        ra_in = lax.ppermute(ra, both, a_route)
        rb_in = lax.ppermute(rb, both, b_route)
        near_in = lax.ppermute(near, "lon", near_route)
        far_in = lax.ppermute(far, "lon", far_route)
    with jax.named_scope("inside"):
        *base, pin, p62, p1 = pl.pallas_call(
            main_kernel,
            in_specs=[VM] * 5,
            out_specs=[VM] * 7,
            out_shape=[vfield] * 4 + [pltpu.VMEM((NK, NI), F32)] * 3,
            scratch_shapes=[pltpu.VMEM((NJ, NI), F32)] * 7,
            compiler_params=params,
            cost_estimate=pl.CostEstimate(
                flops=40_000_000, bytes_accessed=13_000_000, transcendentals=0
            ),
        )(kmt, *held)
    base = [near_core(x) for x in base]
    rest = [near_core(x) for x in (pin, p62, p1, near, far, near_in, far_in, ra_in, rb_in)]
    with jax.named_scope("edges"):
        return tuple(
            x.reshape(NK, NJ, NI)
            for x in pl.pallas_call(
                fix_kernel,
                in_specs=[VM] * 18,
                out_specs=[ANY] * 4,
                out_shape=[field] * 4,
                scratch_shapes=[
                    pltpu.VMEM((4, NK * NJ, NI), F32),
                    pltpu.VMEM((2, 4, NK, NI), F32),
                    pltpu.SemaphoreType.DMA((CH, 4)),
                ],
                compiler_params=params,
                cost_estimate=pl.CostEstimate(
                    flops=4_000_000, bytes_accessed=7_000_000, transcendentals=0
                ),
            )(kmt, *held, *base, *rest)
        )


def solution(mesh):
    grid = P(None, "lat", "lon")
    return jax.shard_map(
        shards,
        mesh=mesh,
        in_specs=(grid,) * 4 + (P("lat", "lon"),),
        out_specs=(grid,) * 4,
        check_vma=False,
    )
```

time: 157 us -> 52.8 us (0.34)
  other arithmetic: 76.9 us -> 0 us
  local copies, waits for them, and re-layouts: 41.6 us -> 0 us
  Pallas kernels: 0 us -> 40.2 us
  waiting for transfers between devices: 13.7 us -> 0.01 us
  starting transfers between devices: 23.5 us -> 11.6 us
    mul x6 -> x0, other arithmetic: 51.1 us -> none  [the longest x1 17.2 us: advance(): seawater_indicator * (centre(salt_ext) - time_step * divergence(salt_ext))]
    pallas_call x0 -> x3, Pallas kernels: none -> 40.2 us  [the longest x1 28.9 us: shards(): pl.pallas_call(main_kernel, in_specs=[VM] * 5, out_specs=[VM] * 7, out_sh...]
    concatenate x2 -> x0, other arithmetic: 19.8 us -> none  [the longest x1 19.8 us: padded_2(): jnp.concatenate([lax.ppermute(tail, axis, [(i, (i + 1) % count) for i in...]
    slice x4 -> x0, local copies, waits for them, and re-layouts: 18.2 us -> none  [the longest x3 12.9 us: padded_2(): lax.slice_in_dim(cells, cells.shape[dim] - width, cells.shape[dim], axis=...]
    ppermute x9 -> x4, waiting for transfers between devices: 13.7 us -> 0.01 us  [the longest x1 0.01 us: shards(): near_in = lax.ppermute(near, 'lon', near_route)]
    ppermute x9 -> x4, starting transfers between devices: 23.5 us -> 11.6 us  [the longest x1 7.99 us: shards(): far_in = lax.ppermute(far, 'lon', far_route)]
    ppermute x3 -> x0, local copies, waits for them, and re-layouts: 10 us -> none  [the longest x2 5.06 us: padded_2(): lax.ppermute(head, axis, [((i + 1) % count, i) for i in range(ends)])]
    scatter x1 -> x0, local copies, waits for them, and re-layouts: 6.84 us -> none  [extend_tile(): return padded.at[:, -1, :].set(new_row)]
  transfers between devices with their start and end apart: 9 -> 4, of which waited for: 3 -> 0; matrix products, arithmetic and copies ran while one was open for 20% -> 0% of each run, Pallas kernels for 0% -> 55%
where the time goes in v1:
time: 52.8 us; the launch traced here: 52.5 us
  Pallas kernels  40.2 us (76%)
  starting transfers between devices  11.6 us (22%)
  between operations  0.67 us (1%)
    pallas_call x1, Pallas kernels, shards(): pl.pallas_call(main_kernel, in_specs=[VM] * 5, out_specs=[VM] * 7, out_sh...  28.9 us
    ppermute x1, starting transfers between devices, shards(): far_in = lax.ppermute(far, 'lon', far_route)  7.99 us
    pallas_call x1, Pallas kernels, shards(): pl.pallas_call(fix_kernel, in_specs=[VM] * 18, out_specs=[ANY] * 4, out_s...  5.74 us
    pallas_call x1, Pallas kernels, shards(): pl.pallas_call(pack_kernel, in_specs=[VM] + [ANY] * 4, out_specs=[VM] * 8...  5.58 us
    ppermute x1, starting transfers between devices, shards(): rb_in = lax.ppermute(rb, both, b_route)  1.98 us
    ppermute x1, starting transfers between devices, shards(): ra_in = lax.ppermute(ra, both, a_route)  1.58 us
  transfers between devices with their start and end apart: 4, of which 0 were waited for; matrix products, arithmetic and copies ran while one was open for 0% of the time, Pallas kernels for 55%

profile of v1, /device:TPU:8, one launch (start us, length us, event | category | flops | bytes accessed | tf_op | source)
XLA Modules:
  0.0 52.5 jit_solution(12160244431048454468)
XLA Ops:
  0.6 5.6 %pack.1 = (f32[3072,128]{1,0:T(8,128)S(1)}, f32[3072,128]{1,0:T(8,128)S(1)}, f32[3072,128]{1,0:T(8,128)S(1)}, f32[3072,128]{1,0:T(8,128)S(1)}, f32[112,128]{1,0:...) custom-call(s32[64,128]{1,0:T(8,128)} %kmt.5, f32[3072,128]{1,0:T(8,128)} %bitcast.8, ...), custom_call_target="tpu_custom_call" | custom-call | flops 4000000 | bytes 7000000 | tf_op jit(solution)/shard_map/pack/pallas_call | solution.py:388
  6.2 1.6 %collective-permute-start.2 = (f32[200,128]{1,0:T(8,128)S(1)}, f32[200,128]{1,0:T(8,128)S(1)}, u32[]{:S(2)}, u32[]{:S(2)}) collective-permute-start(f32[200,128]{1,0:T(8,128)S(1)} %get-tuple-element.36), channel_id=1, source_target_pairs={{0,1},{1,0},{2,3},{3,2},{4,5},{5,4},{6,7},{7,6},{8,9},{9,8},{10,11... | collective-permute-start | bytes 307208 | tf_op jit(solution)/shard_map/halo/ppermute | solution.py:419
  7.8 2.0 %collective-permute-start.3 = (f32[200,128]{1,0:T(8,128)S(1)}, f32[200,128]{1,0:T(8,128)S(1)}, u32[]{:S(2)}, u32[]{:S(2)}) collective-permute-start(f32[200,128]{1,0:T(8,128)S(1)} %get-tuple-element.37), channel_id=1, source_target_pairs={{0,8},{1,2},{2,1},{3,4},{4,3},{5,6},{6,5},{7,255},{8,0},{9,10},{10... | collective-permute-start | bytes 307208 | tf_op jit(solution)/shard_map/halo/ppermute | solution.py:420
  9.8 0.0 collective-permute-start
  9.8 8.0 %collective-permute-start.1 = (f32[112,128]{1,0:T(8,128)S(1)}, f32[112,128]{1,0:T(8,128)S(1)}, u32[]{:S(2)}, u32[]{:S(2)}) collective-permute-start(f32[112,128]{1,0:T(8,128)S(1)} %get-tuple-element.35.far), channel_id=1, source_target_pairs={{0,248},{8,16},{16,8},{24,32},{32,24},{40,48},{48,40},{56,64},{64,... | collective-permute-start | bytes 172040 | tf_op jit(solution)/shard_map/halo/ppermute | solution.py:422
  17.8 28.9 %inside.1 = (f32[3072,128]{1,0:T(8,128)S(1)}, f32[3072,128]{1,0:T(8,128)S(1)}, f32[3072,128]{1,0:T(8,128)S(1)}, f32[3072,128]{1,0:T(8,128)S(1)}, f32[48,128]{1,0...) custom-call(s32[64,128]{1,0:T(8,128)} %kmt.5, f32[3072,128]{1,0:T(8,128)S(1)} %get-tuple-element.23.u_ref, ...), custom_call_target="tpu_custom_call" | custom-call | flops 40000000 | bytes 13000000 | tf_op jit(solution)/shard_map/inside/pallas_call | solution.py:424
  46.7 0.0 collective-permute-done.near_in
  46.7 0.0 collective-permute-done.1.far_in
  46.7 0.0 collective-permute-done.2.ra_in
  46.7 0.0 collective-permute-done.3.rb_in
  46.7 5.7 %edges.1 = (f32[3072,128]{1,0:T(8,128)}, f32[3072,128]{1,0:T(8,128)}, f32[3072,128]{1,0:T(8,128)}, f32[3072,128]{1,0:T(8,128)}) custom-call(s32[64,128]{1,0:T(8,128)} %kmt.5, f32[3072,128]{1,0:T(8,128)S(1)} %get-tuple-element.23.u_ref, f32[3072,128]{1,0:T(8,128)S(1)} %get-tuple-element.24.v_ref, f32[3072,128]{1,0:T(8,128)S(1)} %get-tuple-element.25.t_ref, ...), custom_call_target="tpu_custom_call" | custom-call | flops 4000000 | bytes 7000000 | tf_op jit(solution)/shard_map/edges/pallas_call | solution.py:440
Async XLA Ops:
  6.2 40.5 %collective-permute-start.2 = (f32[200,128]{1,0:T(8,128)S(1)}, f32[200,128]{1,0:T(8,128)S(1)}, u32[]{:S(2)}, u32[]{:S(2)}) collective-permute-start(f32[200,128]{1,0:T(8,128)S(1)} %get-tuple-element.36), channel_id=1, source_target_pairs={{0,1},{1,0},{2,3},{3,2},{4,5},{5,4},{6,7},{7,6},{8,9},{9,8},{10,11... | collective-permute-start | bytes 307208 | tf_op jit(solution)/shard_map/halo/ppermute | solution.py:419
  7.8 38.9 %collective-permute-start.3 = (f32[200,128]{1,0:T(8,128)S(1)}, f32[200,128]{1,0:T(8,128)S(1)}, u32[]{:S(2)}, u32[]{:S(2)}) collective-permute-start(f32[200,128]{1,0:T(8,128)S(1)} %get-tuple-element.37), channel_id=1, source_target_pairs={{0,8},{1,2},{2,1},{3,4},{4,3},{5,6},{6,5},{7,255},{8,0},{9,10},{10... | collective-permute-start | bytes 307208 | tf_op jit(solution)/shard_map/halo/ppermute | solution.py:420
  9.8 36.9 %collective-permute-start = (f32[112,128]{1,0:T(8,128)S(1)}, f32[112,128]{1,0:T(8,128)S(1)}, u32[]{:S(2)}, u32[]{:S(2)}) collective-permute-start(f32[112,128]{1,0:T(8,128)S(1)} %get-tuple-element.34.near), channel_id=1, source_target_pairs={{0,8},{8,0},{16,24},{24,16},{32,40},{40,32},{48,56},{56,48},{64,72... | collective-permute-start | bytes 172040 | tf_op jit(solution)/shard_map/halo/ppermute | solution.py:421
  9.8 36.9 %collective-permute-start.1 = (f32[112,128]{1,0:T(8,128)S(1)}, f32[112,128]{1,0:T(8,128)S(1)}, u32[]{:S(2)}, u32[]{:S(2)}) collective-permute-start(f32[112,128]{1,0:T(8,128)S(1)} %get-tuple-element.35.far), channel_id=1, source_target_pairs={{0,248},{8,16},{16,8},{24,32},{32,24},{40,48},{48,40},{56,64},{64,... | collective-permute-start | bytes 172040 | tf_op jit(solution)/shard_map/halo/ppermute | solution.py:422

commit v2 on v1

--- a/solution.py
+++ b/solution.py
@@ -141,7 +141,7 @@
 
 
 def main_kernel(
-    kmt, u_ref, v_ref, t_ref, s_ref, ou, ov, ot, os, pin, p62, p1, ks, ke, kn, kew, kns, rs, fs
+    kmt, u_ref, v_ref, t_ref, s_ref, ou, ov, ot, os, pin, p62, p1, ks, ke, kn, kew, kns, rs, fs, pins
 ):
     kf = kmt[...].astype(F32)
     lane64 = lax.broadcasted_iota(jnp.int32, (NJ, NI), 1)
@@ -175,7 +175,7 @@
     def south(now, before):
         return roll(jnp.where(row7, before, now), 1, 0)
 
-    def level(k, acc, edge):
+    def level(k, acc):
         kk = k.astype(F32)
         c1, c2, c3 = level_terms(kk)
         press, acc_new = [], []
@@ -188,7 +188,7 @@
             acc_new.append(p + w)
         p62[pl.ds(k, 1), :] = press[JT - 1][6:7, :]
         p1[pl.ds(k, 1), :] = press[0][1:2, :]
-        edge = [roll(x, 120, 1) for x in edge]
+        edge = [zero, zero]
         before = [zero] * 4
         for jt in range(JT):
             q = [tile(ref, k, jt) for ref in (u_ref, v_ref, t_ref, s_ref)]
@@ -219,18 +219,21 @@
             wet = fixed(ks, jt) > kk
             for ref, x in zip((ou, ov, ot, os), out):
                 ref[place(k, jt), :] = jnp.where(wet, x, 0.0)
-        return acc_new, edge
-
-    def step(q, carry):
-        acc = list(carry[:JT])
-        edges = list(carry[JT:])
-        for i in range(3):
-            acc, edges[2 * i : 2 * i + 2] = level(q * 3 + i, acc, edges[2 * i : 2 * i + 2])
-        return tuple(acc) + tuple(edges)
-
-    carry = lax.fori_loop(0, NQ, step, (zero,) * (JT + 6))
+        for half in range(2):
+            pins[pl.ds(pl.multiple_of(k * 16, 16) + 8 * half, 8), :] = edge[half]
+        return tuple(acc_new)
+
+    lax.fori_loop(0, NK, level, (zero,) * JT)
+
+    def gather(q, carry):
+        at = pl.multiple_of(q * 48, 48)
+        return tuple(
+            roll(x, 120, 1) + pins[pl.ds(at + 8 * n, 8), :] for n, x in enumerate(carry)
+        )
+
+    pairs = lax.fori_loop(0, NQ, gather, (zero,) * 6)
     for i in range(3):
-        e, w = split_pairs(carry[JT + 2 * i], carry[JT + 2 * i + 1], even)
+        e, w = split_pairs(pairs[2 * i], pairs[2 * i + 1], even)
         pin[8 * i : 8 * i + 8, :] = e
         pin[24 + 8 * i : 32 + 8 * i, :] = w
 
@@ -426,7 +429,7 @@
             in_specs=[VM] * 5,
             out_specs=[VM] * 7,
             out_shape=[vfield] * 4 + [pltpu.VMEM((NK, NI), F32)] * 3,
-            scratch_shapes=[pltpu.VMEM((NJ, NI), F32)] * 7,
+            scratch_shapes=[pltpu.VMEM((NJ, NI), F32)] * 7 + [pltpu.VMEM((NK * 16, NI), F32)],
             compiler_params=params,
             cost_estimate=pl.CostEstimate(
                 flops=40_000_000, bytes_accessed=13_000_000, transcendentals=0

time: 52.8 us -> 35.1 us (0.66)
  Pallas kernels: 40.2 us -> 22.6 us
    pallas_call x1, Pallas kernels: 28.9 us -> 11.3 us  [shards(): pl.pallas_call(main_kernel, in_specs=[VM] * 5, out_specs=[VM] * 7, out_sh...]
  transfers between devices with their start and end apart: 4 -> 4, of which waited for: 0 -> 0; matrix products, arithmetic and copies ran while one was open for 0% -> 0% of each run, Pallas kernels for 55% -> 32%
where the time goes in v2:
time: 35.1 us; the launch traced here: 34.8 us
  Pallas kernels  22.6 us (64%)
  starting transfers between devices  11.6 us (33%)
  between operations  0.67 us (2%)
    pallas_call x1, Pallas kernels, shards(): pl.pallas_call(main_kernel, in_specs=[VM] * 5, out_specs=[VM] * 7, out_sh...  11.3 us
    ppermute x1, starting transfers between devices, shards(): far_in = lax.ppermute(far, 'lon', far_route)  7.99 us
    pallas_call x1, Pallas kernels, shards(): pl.pallas_call(fix_kernel, in_specs=[VM] * 18, out_specs=[ANY] * 4, out_s...  5.74 us
    pallas_call x1, Pallas kernels, shards(): pl.pallas_call(pack_kernel, in_specs=[VM] + [ANY] * 4, out_specs=[VM] * 8...  5.58 us
    ppermute x1, starting transfers between devices, shards(): rb_in = lax.ppermute(rb, both, b_route)  1.98 us
    ppermute x1, starting transfers between devices, shards(): ra_in = lax.ppermute(ra, both, a_route)  1.58 us
  transfers between devices with their start and end apart: 4, of which 0 were waited for; matrix products, arithmetic and copies ran while one was open for 0% of the time, Pallas kernels for 32%

profile of v2, /device:TPU:8, one launch (start us, length us, event | category | flops | bytes accessed | tf_op | source)
XLA Modules:
  0.0 34.8 jit_solution(15390729237248057210)
XLA Ops:
  0.6 5.6 %pack.1 = (f32[3072,128]{1,0:T(8,128)S(1)}, f32[3072,128]{1,0:T(8,128)S(1)}, f32[3072,128]{1,0:T(8,128)S(1)}, f32[3072,128]{1,0:T(8,128)S(1)}, f32[112,128]{1,0:...) custom-call(s32[64,128]{1,0:T(8,128)} %kmt.5, f32[3072,128]{1,0:T(8,128)} %bitcast.8, ...), custom_call_target="tpu_custom_call" | custom-call | flops 4000000 | bytes 7000000 | tf_op jit(solution)/shard_map/pack/pallas_call | solution.py:391
  6.2 1.6 %collective-permute-start.2 = (f32[200,128]{1,0:T(8,128)S(1)}, f32[200,128]{1,0:T(8,128)S(1)}, u32[]{:S(2)}, u32[]{:S(2)}) collective-permute-start(f32[200,128]{1,0:T(8,128)S(1)} %get-tuple-element.36), channel_id=1, source_target_pairs={{0,1},{1,0},{2,3},{3,2},{4,5},{5,4},{6,7},{7,6},{8,9},{9,8},{10,11... | collective-permute-start | bytes 307208 | tf_op jit(solution)/shard_map/halo/ppermute | solution.py:422
  7.8 2.0 %collective-permute-start.3 = (f32[200,128]{1,0:T(8,128)S(1)}, f32[200,128]{1,0:T(8,128)S(1)}, u32[]{:S(2)}, u32[]{:S(2)}) collective-permute-start(f32[200,128]{1,0:T(8,128)S(1)} %get-tuple-element.37), channel_id=1, source_target_pairs={{0,8},{1,2},{2,1},{3,4},{4,3},{5,6},{6,5},{7,255},{8,0},{9,10},{10... | collective-permute-start | bytes 307208 | tf_op jit(solution)/shard_map/halo/ppermute | solution.py:423
  9.8 0.0 collective-permute-start
  9.8 8.0 %collective-permute-start.1 = (f32[112,128]{1,0:T(8,128)S(1)}, f32[112,128]{1,0:T(8,128)S(1)}, u32[]{:S(2)}, u32[]{:S(2)}) collective-permute-start(f32[112,128]{1,0:T(8,128)S(1)} %get-tuple-element.35.far), channel_id=1, source_target_pairs={{0,248},{8,16},{16,8},{24,32},{32,24},{40,48},{48,40},{56,64},{64,... | collective-permute-start | bytes 172040 | tf_op jit(solution)/shard_map/halo/ppermute | solution.py:425
  17.8 11.3 %inside.1 = (f32[3072,128]{1,0:T(8,128)S(1)}, f32[3072,128]{1,0:T(8,128)S(1)}, f32[3072,128]{1,0:T(8,128)S(1)}, f32[3072,128]{1,0:T(8,128)S(1)}, f32[48,128]{1,0...) custom-call(s32[64,128]{1,0:T(8,128)} %kmt.5, f32[3072,128]{1,0:T(8,128)S(1)} %get-tuple-element.23.u_ref, ...), custom_call_target="tpu_custom_call" | custom-call | flops 40000000 | bytes 13000000 | tf_op jit(solution)/shard_map/inside/pallas_call | solution.py:427
  29.0 0.0 collective-permute-done.near_in
  29.0 0.0 collective-permute-done.1.far_in
  29.1 0.0 collective-permute-done.2.ra_in
  29.1 0.0 collective-permute-done.3.rb_in
  29.1 5.7 %edges.1 = (f32[3072,128]{1,0:T(8,128)}, f32[3072,128]{1,0:T(8,128)}, f32[3072,128]{1,0:T(8,128)}, f32[3072,128]{1,0:T(8,128)}) custom-call(s32[64,128]{1,0:T(8,128)} %kmt.5, f32[3072,128]{1,0:T(8,128)S(1)} %get-tuple-element.23.u_ref, f32[3072,128]{1,0:T(8,128)S(1)} %get-tuple-element.24.v_ref, f32[3072,128]{1,0:T(8,128)S(1)} %get-tuple-element.25.t_ref, ...), custom_call_target="tpu_custom_call" | custom-call | flops 4000000 | bytes 7000000 | tf_op jit(solution)/shard_map/edges/pallas_call | solution.py:443
Async XLA Ops:
  6.2 22.9 %collective-permute-start.2 = (f32[200,128]{1,0:T(8,128)S(1)}, f32[200,128]{1,0:T(8,128)S(1)}, u32[]{:S(2)}, u32[]{:S(2)}) collective-permute-start(f32[200,128]{1,0:T(8,128)S(1)} %get-tuple-element.36), channel_id=1, source_target_pairs={{0,1},{1,0},{2,3},{3,2},{4,5},{5,4},{6,7},{7,6},{8,9},{9,8},{10,11... | collective-permute-start | bytes 307208 | tf_op jit(solution)/shard_map/halo/ppermute | solution.py:422
  7.8 21.3 %collective-permute-start.3 = (f32[200,128]{1,0:T(8,128)S(1)}, f32[200,128]{1,0:T(8,128)S(1)}, u32[]{:S(2)}, u32[]{:S(2)}) collective-permute-start(f32[200,128]{1,0:T(8,128)S(1)} %get-tuple-element.37), channel_id=1, source_target_pairs={{0,8},{1,2},{2,1},{3,4},{4,3},{5,6},{6,5},{7,255},{8,0},{9,10},{10... | collective-permute-start | bytes 307208 | tf_op jit(solution)/shard_map/halo/ppermute | solution.py:423
  9.8 19.3 %collective-permute-start = (f32[112,128]{1,0:T(8,128)S(1)}, f32[112,128]{1,0:T(8,128)S(1)}, u32[]{:S(2)}, u32[]{:S(2)}) collective-permute-start(f32[112,128]{1,0:T(8,128)S(1)} %get-tuple-element.34.near), channel_id=1, source_target_pairs={{0,8},{8,0},{16,24},{24,16},{32,40},{40,32},{48,56},{56,48},{64,72... | collective-permute-start | bytes 172040 | tf_op jit(solution)/shard_map/halo/ppermute | solution.py:424
  9.8 19.3 %collective-permute-start.1 = (f32[112,128]{1,0:T(8,128)S(1)}, f32[112,128]{1,0:T(8,128)S(1)}, u32[]{:S(2)}, u32[]{:S(2)}) collective-permute-start(f32[112,128]{1,0:T(8,128)S(1)} %get-tuple-element.35.far), channel_id=1, source_target_pairs={{0,248},{8,16},{16,8},{24,32},{32,24},{40,48},{48,40},{56,64},{64,... | collective-permute-start | bytes 172040 | tf_op jit(solution)/shard_map/halo/ppermute | solution.py:425

commit v3 on v2

--- a/solution.py
+++ b/solution.py
@@ -114,7 +114,7 @@
     for c in range(CH):
         for copy in copies[c]:
             copy.wait()
-        carry = lax.fori_loop(c * NQ // CH, (c + 1) * NQ // CH, step, carry)
+        carry = lax.fori_loop(c * NQ // CH, (c + 1) * NQ // CH, step, carry, unroll=4)
     for f in range(4):
         for i in range(3):
             e, w = split_pairs(carry[f * 6 + i * 2], carry[f * 6 + i * 2 + 1], even)
@@ -141,7 +141,7 @@
 
 
 def main_kernel(
-    kmt, u_ref, v_ref, t_ref, s_ref, ou, ov, ot, os, pin, p62, p1, ks, ke, kn, kew, kns, rs, fs, pins
+    kmt, u_ref, v_ref, t_ref, s_ref, ou, ov, ot, os, pin, p62, p1, ks, ke, kn, kew, kns, rs, fs, pins, press, flux, rise, inner
 ):
     kf = kmt[...].astype(F32)
     lane64 = lax.broadcasted_iota(jnp.int32, (NJ, NI), 1)
@@ -161,7 +161,7 @@
         fs[8 * jt : 8 * jt + 8, :] = jnp.broadcast_to(0.1 * f[:, jt : jt + 1], (8, NI))
 
     lane, row = lanes(), subs()
-    first, row0, row7 = lane == 0, row == 0, row == 7
+    first = lane == 0
     even = (lane & 1) == 0
     spot = [(lane >> 1) == 60 + jh for jh in range(4)]
     zero = jnp.zeros((8, NI), F32)
@@ -169,64 +169,83 @@
     def fixed(ref, jt):
         return ref[8 * jt : 8 * jt + 8, :]
 
-    def north(now, after):
-        return roll(jnp.where(row0, after, now), 7, 0)
-
-    def south(now, before):
-        return roll(jnp.where(row7, before, now), 1, 0)
-
-    def level(k, acc):
+    def after(ref, x, k, jt):
+        if jt == JT - 1:
+            return roll(x, 7, 0)
+        return ref[pl.ds(pl.multiple_of(k * NJ, NJ) + 8 * jt + 1, 8), :]
+
+    fields, outs = (u_ref, v_ref, t_ref, s_ref), (ou, ov, ot, os)
+
+    def open_level(k, acc):
         kk = k.astype(F32)
         c1, c2, c3 = level_terms(kk)
-        press, acc_new = [], []
+        acc_new = []
         for jt in range(JT):
-            t = tile(t_ref, k, jt)
-            w = t * (c1 + c2 * t) + c3 * tile(s_ref, k, jt)
+            q = [tile(ref, k, jt) for ref in fields]
+            w = q[2] * (c1 + c2 * q[2]) + c3 * q[3]
             w = jnp.where(fixed(ks, jt) > kk, w, 0.0)
             p = acc[jt] + w
-            press.append(p)
+            press[8 + 8 * jt : 16 + 8 * jt, :] = p
             acc_new.append(p + w)
-        p62[pl.ds(k, 1), :] = press[JT - 1][6:7, :]
-        p1[pl.ds(k, 1), :] = press[0][1:2, :]
-        edge = [zero, zero]
-        before = [zero] * 4
+            qe = [x + roll(x, 127, 1) for x in q]
+            flow = jnp.where(fixed(ke, jt) > kk, fixed(rs, jt), 0.0) * qe[0]
+            for f in range(4):
+                flux[f, 8 * jt : 8 * jt + 8, :] = flow * qe[f]
+            qn = [x + after(ref, x, k, jt) for x, ref in zip(q, fields)]
+            flow = jnp.where(fixed(kn, jt) > kk, 0.025, 0.0) * qn[1]
+            for f in range(4):
+                rise[f, 8 + 8 * jt : 16 + 8 * jt, :] = flow * qn[f]
+        return tuple(acc_new)
+
+    def close_level(k):
+        kk = k.astype(F32)
+        p62[pl.ds(k, 1), :] = press[8 + NJ - 2 : 8 + NJ - 1, :]
+        p1[pl.ds(k, 1), :] = press[9:10, :]
         for jt in range(JT):
-            q = [tile(ref, k, jt) for ref in (u_ref, v_ref, t_ref, s_ref)]
-            up = min(jt + 1, JT - 1)
-            r25, f01 = fixed(rs, jt), fixed(fs, jt)
-            qe = [x + roll(x, 127, 1) for x in q]
-            flow = jnp.where(fixed(ke, jt) > kk, r25, 0.0) * qe[0]
-            fe = [flow * x for x in qe]
-            qn = [
-                x + north(x, tile(ref, k, up)) for x, ref in zip(q, (u_ref, v_ref, t_ref, s_ref))
+            q = [tile(ref, k, jt) for ref in fields]
+            f01 = fixed(fs, jt)
+            fe = [flux[f, 8 * jt : 8 * jt + 8, :] for f in range(4)]
+            fn = [rise[f, 8 + 8 * jt : 16 + 8 * jt, :] for f in range(4)]
+            fs_ = [rise[f, 7 + 8 * jt : 15 + 8 * jt, :] for f in range(4)]
+            out = [
+                x - (a - roll(a, 1, 1)) - (b - c) for x, a, b, c in zip(q, fe, fn, fs_)
             ]
-            flow = jnp.where(fixed(kn, jt) > kk, 0.025, 0.0) * qn[1]
-            fn = [flow * x for x in qn]
-            out = [
-                x - (a - roll(a, 1, 1)) - (b - south(b, c))
-                for x, a, b, c in zip(q, fe, fn, before)
-            ]
-            before = fn
-            p = press[jt]
+            p = press[8 + 8 * jt : 16 + 8 * jt, :]
             pe, pw = roll(p, 127, 1), roll(p, 1, 1)
-            spot_p = roll(jnp.where(first, pe, pw), 121 + 2 * (jt // 2), 1)
-            edge[jt % 2] = jnp.where(spot[jt // 2], spot_p, edge[jt % 2])
-            slope = jnp.where(fixed(kew, jt) > kk, 2.0 * r25, 0.0) * (pe - pw)
+            inner[8 * jt : 8 * jt + 8, :] = jnp.where(first, pe, pw)
+            slope = jnp.where(fixed(kew, jt) > kk, 2.0 * fixed(rs, jt), 0.0) * (pe - pw)
             out[0] = out[0] + (f01 * q[1] - slope)
-            pn, ps = north(p, press[up]), south(p, press[max(jt - 1, 0)])
+            pn = press[9 + 8 * jt : 17 + 8 * jt, :]
+            ps = press[7 + 8 * jt : 15 + 8 * jt, :]
             slope = jnp.where(fixed(kns, jt) > kk, 0.05, 0.0) * (pn - ps)
             out[1] = out[1] - (f01 * q[0] + slope)
             wet = fixed(ks, jt) > kk
-            for ref, x in zip((ou, ov, ot, os), out):
+            for ref, x in zip(outs, out):
                 ref[place(k, jt), :] = jnp.where(wet, x, 0.0)
+
+    def pack_inner(k):
         for half in range(2):
-            pins[pl.ds(pl.multiple_of(k * 16, 16) + 8 * half, 8), :] = edge[half]
-        return tuple(acc_new)
-
-    lax.fori_loop(0, NK, level, (zero,) * JT)
+            edge = zero
+            for jh in range(4):
+                x = roll(fixed(inner, 2 * jh + half), 121 + 2 * jh, 1)
+                edge = jnp.where(spot[jh], x, edge)
+            pins[pl.ds(pl.multiple_of(k * 16, 16) + 8 * half, 8), :] = edge
+
+    def level(k, acc):
+        pack_inner(k)
+        close_level(k)
+        return open_level(jnp.minimum(k + 1, NK - 1), acc)
+
+    inner[...] = jnp.zeros((NJ, NI), F32)
+    press[0:8, :] = zero
+    press[8 + NJ : 16 + NJ, :] = zero
+    for f in range(4):
+        rise[f, 0:8, :] = zero
+    lax.fori_loop(0, NK, level, open_level(jnp.int32(0), (zero,) * JT))
+    pack_inner(jnp.int32(NK))
 
     def gather(q, carry):
-        at = pl.multiple_of(q * 48, 48)
+        at = pl.multiple_of(q * 48, 16) + 16
         return tuple(
             roll(x, 120, 1) + pins[pl.ds(at + 8 * n, 8), :] for n, x in enumerate(carry)
         )
@@ -362,7 +381,7 @@
     carry = tuple(packs)
     copies = []
     for c in range(CH):
-        carry = lax.fori_loop(c * NQ // CH, (c + 1) * NQ // CH, step, carry)
+        carry = lax.fori_loop(c * NQ // CH, (c + 1) * NQ // CH, step, carry, unroll=4)
         for f in range(4):
             copy = pltpu.make_async_copy(
                 buf.at[f, pl.ds(c * CK * NJ, CK * NJ)],
@@ -429,7 +448,13 @@
             in_specs=[VM] * 5,
             out_specs=[VM] * 7,
             out_shape=[vfield] * 4 + [pltpu.VMEM((NK, NI), F32)] * 3,
-            scratch_shapes=[pltpu.VMEM((NJ, NI), F32)] * 7 + [pltpu.VMEM((NK * 16, NI), F32)],
+            scratch_shapes=[pltpu.VMEM((NJ, NI), F32)] * 7 + [
+                pltpu.VMEM((NK * 16 + 16, NI), F32),
+                pltpu.VMEM((NJ + 16, NI), F32),
+                pltpu.VMEM((4, NJ, NI), F32),
+                pltpu.VMEM((4, NJ + 8, NI), F32),
+                pltpu.VMEM((NJ, NI), F32),
+            ],
             compiler_params=params,
             cost_estimate=pl.CostEstimate(
                 flops=40_000_000, bytes_accessed=13_000_000, transcendentals=0

time: 35.1 us -> 31.6 us (0.900)
  Pallas kernels: 22.6 us -> 19.1 us
    pallas_call x1, Pallas kernels: 5.74 us -> 4.44 us  [shards(): pl.pallas_call(fix_kernel, in_specs=[VM] * 18, out_specs=[ANY] * 4, out_s...]
    pallas_call x1, Pallas kernels: 11.3 us -> 9.96 us  [shards(): pl.pallas_call(main_kernel, in_specs=[VM] * 5, out_specs=[VM] * 7, out_sh...]
    pallas_call x1, Pallas kernels: 5.58 us -> 4.68 us  [shards(): pl.pallas_call(pack_kernel, in_specs=[VM] + [ANY] * 4, out_specs=[VM] * 8...]
where the time goes in v3:
time: 31.6 us; the launch traced here: 31.4 us
  Pallas kernels  19.1 us (60%)
  starting transfers between devices  11.6 us (37%)
  between operations  0.67 us (2%)
    pallas_call x1, Pallas kernels, shards(): pl.pallas_call(main_kernel, in_specs=[VM] * 5, out_specs=[VM] * 7, out_sh...  9.96 us
    ppermute x1, starting transfers between devices, shards(): far_in = lax.ppermute(far, 'lon', far_route)  7.99 us
    pallas_call x1, Pallas kernels, shards(): pl.pallas_call(pack_kernel, in_specs=[VM] + [ANY] * 4, out_specs=[VM] * 8...  4.68 us
    pallas_call x1, Pallas kernels, shards(): pl.pallas_call(fix_kernel, in_specs=[VM] * 18, out_specs=[ANY] * 4, out_s...  4.44 us
    ppermute x1, starting transfers between devices, shards(): rb_in = lax.ppermute(rb, both, b_route)  1.98 us
    ppermute x1, starting transfers between devices, shards(): ra_in = lax.ppermute(ra, both, a_route)  1.58 us
  transfers between devices with their start and end apart: 4, of which 0 were waited for; matrix products, arithmetic and copies ran while one was open for 0% of the time, Pallas kernels for 32%

profile of v3, /device:TPU:8, one launch (start us, length us, event | category | flops | bytes accessed | tf_op | source)
XLA Modules:
  0.0 31.4 jit_solution(4367925186304178832)
XLA Ops:
  0.6 4.7 %pack.1 = (f32[3072,128]{1,0:T(8,128)S(1)}, f32[3072,128]{1,0:T(8,128)S(1)}, f32[3072,128]{1,0:T(8,128)S(1)}, f32[3072,128]{1,0:T(8,128)S(1)}, f32[112,128]{1,0:...) custom-call(s32[64,128]{1,0:T(8,128)} %kmt.5, f32[3072,128]{1,0:T(8,128)} %bitcast.8, ...), custom_call_target="tpu_custom_call" | custom-call | flops 4000000 | bytes 7000000 | tf_op jit(solution)/shard_map/pack/pallas_call | solution.py:410
  5.3 1.6 %collective-permute-start.2 = (f32[200,128]{1,0:T(8,128)S(1)}, f32[200,128]{1,0:T(8,128)S(1)}, u32[]{:S(2)}, u32[]{:S(2)}) collective-permute-start(f32[200,128]{1,0:T(8,128)S(1)} %get-tuple-element.36), channel_id=1, source_target_pairs={{0,1},{1,0},{2,3},{3,2},{4,5},{5,4},{6,7},{7,6},{8,9},{9,8},{10,11... | collective-permute-start | bytes 307208 | tf_op jit(solution)/shard_map/halo/ppermute | solution.py:441
  6.9 2.0 %collective-permute-start.3 = (f32[200,128]{1,0:T(8,128)S(1)}, f32[200,128]{1,0:T(8,128)S(1)}, u32[]{:S(2)}, u32[]{:S(2)}) collective-permute-start(f32[200,128]{1,0:T(8,128)S(1)} %get-tuple-element.37), channel_id=1, source_target_pairs={{0,8},{1,2},{2,1},{3,4},{4,3},{5,6},{6,5},{7,255},{8,0},{9,10},{10... | collective-permute-start | bytes 307208 | tf_op jit(solution)/shard_map/halo/ppermute | solution.py:442
  8.9 0.0 collective-permute-start
  8.9 8.0 %collective-permute-start.1 = (f32[112,128]{1,0:T(8,128)S(1)}, f32[112,128]{1,0:T(8,128)S(1)}, u32[]{:S(2)}, u32[]{:S(2)}) collective-permute-start(f32[112,128]{1,0:T(8,128)S(1)} %get-tuple-element.35.far), channel_id=1, source_target_pairs={{0,248},{8,16},{16,8},{24,32},{32,24},{40,48},{48,40},{56,64},{64,... | collective-permute-start | bytes 172040 | tf_op jit(solution)/shard_map/halo/ppermute | solution.py:444
  16.9 10.0 %inside.1 = (f32[3072,128]{1,0:T(8,128)S(1)}, f32[3072,128]{1,0:T(8,128)S(1)}, f32[3072,128]{1,0:T(8,128)S(1)}, f32[3072,128]{1,0:T(8,128)S(1)}, f32[48,128]{1,0...) custom-call(s32[64,128]{1,0:T(8,128)} %kmt.5, f32[3072,128]{1,0:T(8,128)S(1)} %get-tuple-element.23.u_ref, ...), custom_call_target="tpu_custom_call" | custom-call | flops 40000000 | bytes 13000000 | tf_op jit(solution)/shard_map/inside/pallas_call | solution.py:446
  26.8 0.0 collective-permute-done.near_in
  26.8 0.0 collective-permute-done.1.far_in
  26.9 0.0 collective-permute-done.2.ra_in
  26.9 0.0 collective-permute-done.3.rb_in
  26.9 4.4 %edges.1 = (f32[3072,128]{1,0:T(8,128)}, f32[3072,128]{1,0:T(8,128)}, f32[3072,128]{1,0:T(8,128)}, f32[3072,128]{1,0:T(8,128)}) custom-call(s32[64,128]{1,0:T(8,128)} %kmt.5, f32[3072,128]{1,0:T(8,128)S(1)} %get-tuple-element.23.u_ref, f32[3072,128]{1,0:T(8,128)S(1)} %get-tuple-element.24.v_ref, f32[3072,128]{1,0:T(8,128)S(1)} %get-tuple-element.25.t_ref, ...), custom_call_target="tpu_custom_call" | custom-call | flops 4000000 | bytes 7000000 | tf_op jit(solution)/shard_map/edges/pallas_call | solution.py:468
Async XLA Ops:
  5.3 21.6 %collective-permute-start.2 = (f32[200,128]{1,0:T(8,128)S(1)}, f32[200,128]{1,0:T(8,128)S(1)}, u32[]{:S(2)}, u32[]{:S(2)}) collective-permute-start(f32[200,128]{1,0:T(8,128)S(1)} %get-tuple-element.36), channel_id=1, source_target_pairs={{0,1},{1,0},{2,3},{3,2},{4,5},{5,4},{6,7},{7,6},{8,9},{9,8},{10,11... | collective-permute-start | bytes 307208 | tf_op jit(solution)/shard_map/halo/ppermute | solution.py:441
  6.9 20.0 %collective-permute-start.3 = (f32[200,128]{1,0:T(8,128)S(1)}, f32[200,128]{1,0:T(8,128)S(1)}, u32[]{:S(2)}, u32[]{:S(2)}) collective-permute-start(f32[200,128]{1,0:T(8,128)S(1)} %get-tuple-element.37), channel_id=1, source_target_pairs={{0,8},{1,2},{2,1},{3,4},{4,3},{5,6},{6,5},{7,255},{8,0},{9,10},{10... | collective-permute-start | bytes 307208 | tf_op jit(solution)/shard_map/halo/ppermute | solution.py:442
  8.9 18.0 %collective-permute-start = (f32[112,128]{1,0:T(8,128)S(1)}, f32[112,128]{1,0:T(8,128)S(1)}, u32[]{:S(2)}, u32[]{:S(2)}) collective-permute-start(f32[112,128]{1,0:T(8,128)S(1)} %get-tuple-element.34.near), channel_id=1, source_target_pairs={{0,8},{8,0},{16,24},{24,16},{32,40},{40,32},{48,56},{56,48},{64,72... | collective-permute-start | bytes 172040 | tf_op jit(solution)/shard_map/halo/ppermute | solution.py:443
  8.9 18.0 %collective-permute-start.1 = (f32[112,128]{1,0:T(8,128)S(1)}, f32[112,128]{1,0:T(8,128)S(1)}, u32[]{:S(2)}, u32[]{:S(2)}) collective-permute-start(f32[112,128]{1,0:T(8,128)S(1)} %get-tuple-element.35.far), channel_id=1, source_target_pairs={{0,248},{8,16},{16,8},{24,32},{32,24},{40,48},{48,40},{56,64},{64,... | collective-permute-start | bytes 172040 | tf_op jit(solution)/shard_map/halo/ppermute | solution.py:444

commit v4 on v3

--- a/solution.py
+++ b/solution.py
@@ -241,7 +241,7 @@
     press[8 + NJ : 16 + NJ, :] = zero
     for f in range(4):
         rise[f, 0:8, :] = zero
-    lax.fori_loop(0, NK, level, open_level(jnp.int32(0), (zero,) * JT))
+    lax.fori_loop(0, NK, level, open_level(jnp.int32(0), (zero,) * JT), unroll=2)
     pack_inner(jnp.int32(NK))
 
     def gather(q, carry):

time: 31.6 us -> 30.8 us (0.975)
  Pallas kernels: 19.1 us -> 18.2 us
    pallas_call x1, Pallas kernels: 9.96 us -> 9.08 us  [shards(): pl.pallas_call(main_kernel, in_specs=[VM] * 5, out_specs=[VM] * 7, out_sh...]
  transfers between devices with their start and end apart: 4 -> 4, of which waited for: 0 -> 0; matrix products, arithmetic and copies ran while one was open for 0% -> 0% of each run, Pallas kernels for 32% -> 30%
where the time goes in v4:
time: 30.8 us; the launch traced here: 30.5 us
  Pallas kernels  18.2 us (59%)
  starting transfers between devices  11.6 us (38%)
  between operations  0.67 us (2%)
    pallas_call x1, Pallas kernels, shards(): pl.pallas_call(main_kernel, in_specs=[VM] * 5, out_specs=[VM] * 7, out_sh...  9.08 us
    ppermute x1, starting transfers between devices, shards(): far_in = lax.ppermute(far, 'lon', far_route)  7.99 us
    pallas_call x1, Pallas kernels, shards(): pl.pallas_call(pack_kernel, in_specs=[VM] + [ANY] * 4, out_specs=[VM] * 8...  4.68 us
    pallas_call x1, Pallas kernels, shards(): pl.pallas_call(fix_kernel, in_specs=[VM] * 18, out_specs=[ANY] * 4, out_s...  4.44 us
    ppermute x1, starting transfers between devices, shards(): rb_in = lax.ppermute(rb, both, b_route)  1.98 us
    ppermute x1, starting transfers between devices, shards(): ra_in = lax.ppermute(ra, both, a_route)  1.58 us
  transfers between devices with their start and end apart: 4, of which 0 were waited for; matrix products, arithmetic and copies ran while one was open for 0% of the time, Pallas kernels for 30%

profile of v4, /device:TPU:8, one launch (start us, length us, event | category | flops | bytes accessed | tf_op | source)
XLA Modules:
  0.0 30.5 jit_solution(1553515429422045921)
XLA Ops:
  0.6 4.7 %pack.1 = (f32[3072,128]{1,0:T(8,128)S(1)}, f32[3072,128]{1,0:T(8,128)S(1)}, f32[3072,128]{1,0:T(8,128)S(1)}, f32[3072,128]{1,0:T(8,128)S(1)}, f32[112,128]{1,0:...) custom-call(s32[64,128]{1,0:T(8,128)} %kmt.5, f32[3072,128]{1,0:T(8,128)} %bitcast.8, ...), custom_call_target="tpu_custom_call" | custom-call | flops 4000000 | bytes 7000000 | tf_op jit(solution)/shard_map/pack/pallas_call | solution.py:410
  5.3 1.6 %collective-permute-start.2 = (f32[200,128]{1,0:T(8,128)S(1)}, f32[200,128]{1,0:T(8,128)S(1)}, u32[]{:S(2)}, u32[]{:S(2)}) collective-permute-start(f32[200,128]{1,0:T(8,128)S(1)} %get-tuple-element.36), channel_id=1, source_target_pairs={{0,1},{1,0},{2,3},{3,2},{4,5},{5,4},{6,7},{7,6},{8,9},{9,8},{10,11... | collective-permute-start | bytes 307208 | tf_op jit(solution)/shard_map/halo/ppermute | solution.py:441
  6.9 2.0 %collective-permute-start.3 = (f32[200,128]{1,0:T(8,128)S(1)}, f32[200,128]{1,0:T(8,128)S(1)}, u32[]{:S(2)}, u32[]{:S(2)}) collective-permute-start(f32[200,128]{1,0:T(8,128)S(1)} %get-tuple-element.37), channel_id=1, source_target_pairs={{0,8},{1,2},{2,1},{3,4},{4,3},{5,6},{6,5},{7,255},{8,0},{9,10},{10... | collective-permute-start | bytes 307208 | tf_op jit(solution)/shard_map/halo/ppermute | solution.py:442
  8.9 0.0 collective-permute-start
  8.9 8.0 %collective-permute-start.1 = (f32[112,128]{1,0:T(8,128)S(1)}, f32[112,128]{1,0:T(8,128)S(1)}, u32[]{:S(2)}, u32[]{:S(2)}) collective-permute-start(f32[112,128]{1,0:T(8,128)S(1)} %get-tuple-element.35.far), channel_id=1, source_target_pairs={{0,248},{8,16},{16,8},{24,32},{32,24},{40,48},{48,40},{56,64},{64,... | collective-permute-start | bytes 172040 | tf_op jit(solution)/shard_map/halo/ppermute | solution.py:444
  16.9 9.1 %inside.1 = (f32[3072,128]{1,0:T(8,128)S(1)}, f32[3072,128]{1,0:T(8,128)S(1)}, f32[3072,128]{1,0:T(8,128)S(1)}, f32[3072,128]{1,0:T(8,128)S(1)}, f32[48,128]{1,0...) custom-call(s32[64,128]{1,0:T(8,128)} %kmt.5, f32[3072,128]{1,0:T(8,128)S(1)} %get-tuple-element.23.u_ref, ...), custom_call_target="tpu_custom_call" | custom-call | flops 40000000 | bytes 13000000 | tf_op jit(solution)/shard_map/inside/pallas_call | solution.py:446
  26.0 0.0 collective-permute-done.near_in
  26.0 0.0 collective-permute-done.1.far_in
  26.0 0.0 collective-permute-done.2.ra_in
  26.0 0.0 collective-permute-done.3.rb_in
  26.0 4.4 %edges.1 = (f32[3072,128]{1,0:T(8,128)}, f32[3072,128]{1,0:T(8,128)}, f32[3072,128]{1,0:T(8,128)}, f32[3072,128]{1,0:T(8,128)}) custom-call(s32[64,128]{1,0:T(8,128)} %kmt.5, f32[3072,128]{1,0:T(8,128)S(1)} %get-tuple-element.23.u_ref, f32[3072,128]{1,0:T(8,128)S(1)} %get-tuple-element.24.v_ref, f32[3072,128]{1,0:T(8,128)S(1)} %get-tuple-element.25.t_ref, ...), custom_call_target="tpu_custom_call" | custom-call | flops 4000000 | bytes 7000000 | tf_op jit(solution)/shard_map/edges/pallas_call | solution.py:468
Async XLA Ops:
  5.3 20.7 %collective-permute-start.2 = (f32[200,128]{1,0:T(8,128)S(1)}, f32[200,128]{1,0:T(8,128)S(1)}, u32[]{:S(2)}, u32[]{:S(2)}) collective-permute-start(f32[200,128]{1,0:T(8,128)S(1)} %get-tuple-element.36), channel_id=1, source_target_pairs={{0,1},{1,0},{2,3},{3,2},{4,5},{5,4},{6,7},{7,6},{8,9},{9,8},{10,11... | collective-permute-start | bytes 307208 | tf_op jit(solution)/shard_map/halo/ppermute | solution.py:441
  6.9 19.1 %collective-permute-start.3 = (f32[200,128]{1,0:T(8,128)S(1)}, f32[200,128]{1,0:T(8,128)S(1)}, u32[]{:S(2)}, u32[]{:S(2)}) collective-permute-start(f32[200,128]{1,0:T(8,128)S(1)} %get-tuple-element.37), channel_id=1, source_target_pairs={{0,8},{1,2},{2,1},{3,4},{4,3},{5,6},{6,5},{7,255},{8,0},{9,10},{10... | collective-permute-start | bytes 307208 | tf_op jit(solution)/shard_map/halo/ppermute | solution.py:442
  8.9 17.1 %collective-permute-start = (f32[112,128]{1,0:T(8,128)S(1)}, f32[112,128]{1,0:T(8,128)S(1)}, u32[]{:S(2)}, u32[]{:S(2)}) collective-permute-start(f32[112,128]{1,0:T(8,128)S(1)} %get-tuple-element.34.near), channel_id=1, source_target_pairs={{0,8},{8,0},{16,24},{24,16},{32,40},{40,32},{48,56},{56,48},{64,72... | collective-permute-start | bytes 172040 | tf_op jit(solution)/shard_map/halo/ppermute | solution.py:443
  8.9 17.1 %collective-permute-start.1 = (f32[112,128]{1,0:T(8,128)S(1)}, f32[112,128]{1,0:T(8,128)S(1)}, u32[]{:S(2)}, u32[]{:S(2)}) collective-permute-start(f32[112,128]{1,0:T(8,128)S(1)} %get-tuple-element.35.far), channel_id=1, source_target_pairs={{0,248},{8,16},{16,8},{24,32},{32,24},{40,48},{48,40},{56,64},{64,... | collective-permute-start | bytes 172040 | tf_op jit(solution)/shard_map/halo/ppermute | solution.py:444
